TPU v7x, 128 devices: a whole 4x4x4 slice. The times are simulated.
128 devices in a mesh: role: 2 (over y_hi), tile: 64 (over y_lo, x, z, core).
Axes of the slice: x: 4, y: 4 (y_hi: 2, y_lo: 2; y = y_hi * 2 + y_lo), z: 4, core: 2. Of those that a mesh axis runs over, the one named last changes fastest.
Arguments:
- fields_pair: float32 [2, 512, 65536], P('role', None, 'tile'), may hold values from 0 to 1
- velocity: float32 [65536], P('tile'), may hold values from -0.5 to 0.5
- growth: float32 [65536], P('tile'), may hold values from 0.05 to 0.5
- features: bfloat16 [512, 1024], replicated, may hold values from -6 to 6
- assignment: int32 [512], replicated, may hold values from 0 to 511, each once
- out_pair: float32 [2, 1024, 65536], P('role', None, 'tile'), may hold values from -0.1875 to 0.1875
- hidden_pair: float32 [2, 5, 1024, 1024], P('role', None, 'tile'), may hold values from -0.1875 to 0.1875
Outputs:
- fields_next: float32 [2, 512, 65536], P('role', None, 'tile')
- out_next: float32 [2, 1024, 65536], P('role', None, 'tile')
- hidden_next: float32 [2, 5, 1024, 1024], P('role', None, 'tile')
Inputs may be any that keep to these rules, and one draw needn't show every extreme that they name: `assignment`: a permutation of the 512 members.
All inputs are finite; a program needn't handle non-finite values.
Results may differ from a plain program's by a relative error of at most 0.0022.
The roundings to bfloat16 on the way count: a program that leaves them out, or rounds other values in their place, can miss the bound.
Values may be sent and summed in bfloat16 or wider, within the bound.
No kernel may reach another device: no remote copies, remote signals or barrier semaphores. Data moves between devices by JAX's collectives and lax.ppermute only.
A program may use at most 192 MiB of HBM per device.

v0:
```python
import jax
import jax.numpy as jnp
from jax import lax
from jax.sharding import Mesh
from jax.sharding import PartitionSpec as P

BATCH = 512
TILE = ("tile_0", "tile_1", "tile_2", "tile_3")
momentum_decay = 0.9
step_size = 0.1


def extended(value, sides, width):
    for axis, dim in sides:
        count, length = (lax.axis_size(axis), value.shape[dim])
        up = [(i, (i + 1) % count) for i in range(count)]
        down = [(j, i) for i, j in up]
        last = lax.slice_in_dim(value, length - width, length, axis=dim)
        leading = lax.slice_in_dim(value, 0, width, axis=dim)
        before = lax.ppermute(last, axis, up)
        after = lax.ppermute(leading, axis, down)
        value = jnp.concatenate([before, value, after], axis=dim)
    return value


def from_root(value, axis, root):
    return lax.dynamic_index_in_dim(lax.all_gather(value, axis), root, 0, keepdims=False)


def rows_for(lines, count):
    spare = -lines.shape[0] % count
    if not spare:
        return lines
    return jnp.concatenate([lines, jnp.zeros((spare, *lines.shape[1:]), lines.dtype)])


def from_everyone(value, axis):
    copies = jnp.broadcast_to(value, (lax.axis_size(axis), *value.shape))
    return lax.all_to_all(copies, axis, split_axis=0, concat_axis=0, tiled=True)


def joined_along(parts, dim):
    parts = jnp.moveaxis(parts, 0, dim)
    dims = parts.shape
    return parts.reshape(*dims[:dim], dims[dim] * dims[dim + 1], *dims[dim + 2 :])


def gather_axes(value, axes, dim):
    far, near = axes
    parts = from_everyone(from_everyone(value, far), near)
    return joined_along(parts.swapaxes(0, 1).reshape(-1, *value.shape), dim)


def split_up(value, dim, count):
    before, after = (value.shape[:dim], value.shape[dim + 1 :])
    return jnp.moveaxis(value.reshape(*before, count, -1, *after), dim, 0)


def sent_and_summed(value, axis, dim):
    parts = split_up(value, dim, lax.axis_size(axis))
    arrived = lax.all_to_all(parts, axis, split_axis=0, concat_axis=0, tiled=True)
    return arrived.sum(axis=0)


def summed_rows(value, axes, dim):
    far, near = axes
    own = sent_and_summed(split_up(value, dim, lax.axis_size(far)), near, dim + 1)
    return jnp.sum(lax.all_to_all(own, far, 0, 0, tiled=True), axis=0)


def nested_sum(value, axes):
    lines = value.reshape(-1, value.shape[-1])
    padded = rows_for(lines, lax.axis_size(axes[0]) * lax.axis_size(axes[1]))
    whole = gather_axes(summed_rows(padded, axes, 0), axes, 0)
    return lax.slice_in_dim(whole, 0, len(lines)).reshape(value.shape)


def partner(value, axis, distance):
    return lax.ppermute(value, axis, [(i, i ^ 1 << distance) for i in range(lax.axis_size(axis))])


def guarded(flag, action, *operands):

    def skipped(*values):
        return jax.tree.map(jnp.zeros_like, action(*values))

    return lax.cond(flag, action, skipped, *operands)


def silu_slope(values):
    logistic = jax.nn.sigmoid(values)
    return logistic * (1.0 + values * (1.0 - logistic))


def advance(padded, growth):
    states = padded[:-1]
    velocity_row = padded[-1]
    outflow = (
        jnp.maximum(velocity_row[:-1], 0.0) * states[:, :-1]
        + jnp.minimum(velocity_row[:-1], 0.0) * states[:, 1:]
    )
    carried = states[:, 1:-1] - outflow[:, 1:] + outflow[:, :-1]
    return carried + growth * carried * (1.0 - carried)


def body(fields_pair, velocity, growth, features, assignment, out_pair, hidden_pair):
    solver_side = lax.axis_index("role") == 0
    trainer_side = jnp.logical_not(solver_side)
    own_fields = fields_pair[0]
    own_out = out_pair[0]
    own_hidden = hidden_pair[0]
    layer_count = own_hidden.shape[0]
    unit_rows = own_hidden.shape[1]
    first_unit = lax.axis_index(TILE) * unit_rows
    stacked = jnp.concatenate([own_fields, velocity[None, :]], axis=0)
    padded = extended(stacked, ((TILE, 1),), 1)
    advanced = guarded(solver_side, advance, padded, growth)
    fresh_fields = from_root(advanced, "role", 0)
    out_narrow = own_out.astype(jnp.bfloat16)
    hidden_narrow = own_hidden.astype(jnp.bfloat16)
    full_hidden = lax.all_gather(hidden_narrow, TILE, axis=1, tiled=True)

    def forward(features, full_hidden, out_narrow, target):
        inputs = []
        summed_list = []
        activation = features
        for layer_index in range(layer_count):
            inputs.append(activation)
            summed = jnp.dot(
                activation, full_hidden[layer_index], preferred_element_type=jnp.float32
            )
            summed_list.append(summed)
            activation = jax.nn.silu(summed).astype(jnp.bfloat16)
        predicted = jnp.dot(activation, out_narrow, preferred_element_type=jnp.float32)
        residual = ((predicted - target) / BATCH).astype(jnp.bfloat16)
        grad_out = jnp.dot(activation.T, residual, preferred_element_type=jnp.float32)
        partial_grad = lax.dot_general(
            residual, out_narrow, (((1,), (1,)), ((), ())), preferred_element_type=jnp.float32
        )
        return (jnp.stack(summed_list), jnp.stack(inputs), grad_out, partial_grad)

    summed_all, inputs_all, grad_out, partial_grad = guarded(
        trainer_side, forward, features, full_hidden, out_narrow, own_fields
    )
    upstream = nested_sum(partial_grad, (("tile_0", "tile_1", "tile_2"), "tile_3"))

    def backward(summed_all, inputs_all, upstream, full_hidden, first_unit):
        gradients = []
        for layer_index in reversed(range(layer_count)):
            slope = (upstream * silu_slope(summed_all[layer_index])).astype(jnp.bfloat16)
            own_inputs = lax.dynamic_slice_in_dim(inputs_all[layer_index], first_unit, unit_rows, 1)
            gradients.append(jnp.dot(own_inputs.T, slope, preferred_element_type=jnp.float32))
            if layer_index > 0:
                upstream = lax.dot_general(
                    slope,
                    full_hidden[layer_index],
                    (((1,), (1,)), ((), ())),
                    preferred_element_type=jnp.float32,
                )
        return jnp.stack(gradients[::-1])

    grad_hidden = guarded(
        trainer_side, backward, summed_all, inputs_all, upstream, full_hidden, first_unit
    )
    solver_pack = jnp.concatenate([own_out.reshape(-1), own_hidden.reshape(-1)])
    trainer_pack = jnp.concatenate([grad_out.reshape(-1), grad_hidden.reshape(-1)])
    payload = jnp.where(solver_side, solver_pack, trainer_pack)
    received = partner(payload, "role", 0)
    out_length = own_out.size
    other_out = received[:out_length].reshape(own_out.shape)
    other_hidden = received[out_length:].reshape(own_hidden.shape)
    out_next = jnp.where(
        solver_side,
        momentum_decay * own_out + other_out,
        own_out - step_size * (momentum_decay * other_out + grad_out),
    )
    hidden_next = jnp.where(
        solver_side,
        momentum_decay * own_hidden + other_hidden,
        own_hidden - step_size * (momentum_decay * other_hidden + grad_hidden),
    )
    fields_next = jnp.where(solver_side, advanced, jnp.take(fresh_fields, assignment, axis=0))
    return (fields_next[None], out_next[None], hidden_next[None])


def solution(mesh):
    finer = Mesh(
        mesh.devices.reshape(mesh.shape["role"], 2, 4, 4, 2),
        ("role", "tile_0", "tile_1", "tile_2", "tile_3"),
    )
    in_specs = (
        P("role", None, TILE),
        P(TILE),
        P(TILE),
        P(),
        P(),
        P("role", None, TILE),
        P("role", None, TILE, None),
    )
    out_specs = (P("role", None, TILE), P("role", None, TILE), P("role", None, TILE, None))
    return jax.shard_map(body, mesh=finer, in_specs=in_specs, out_specs=out_specs, check_vma=False)
```

profile of v0, /device:TPU:1, one launch (start us, length us, event | category | flops | bytes accessed | tf_op | source)
XLA Modules:
  0.0 405.7 jit_solution(4291175389253201771)
XLA Ops:
  8.0 0.0 all-gather.4.cloned.1.call-start
  8.0 1.7 bitcast_convert_fusion
  9.7 119.9 %all-gather.4.cloned.1.call-done = bf16[5,1024,1024]{2,1,0:T(8,128)(2,1)} async-done(((bf16[5,16,1024]{2,1,0:T(8,128)(2,1)}), bf16[5,1024,1024]{2,1,0:T(8,128)(2,1)}) %all-gather.4.cloned.1.call-update) | async-done | bytes 10485776 | tf_op jit(solution)/shard_map/all_gather | solution.py:121
  129.7 11.4 %conditional.4 = (f32[5,512,1024]{2,1,0:T(8,128)}, bf16[5,512,1024]{2,1,0:T(8,128)(2,1)}, f32[1024,1024]{1,0:T(8,128)}, f32[512,1024]{1,0:T(8,128)S(1)}, f32[1048576]{0:T(1024)S(1)}) conditional(s32[]{:T(128)} %convert_element_type.57, () %tuple.54, (bf16[5,1024,1024]{2,1,0:T(8,128)(2,1)}, bf16[512,1024]{1,0:T(8,128)(2,1)}, f32[1024,1024]{1,0:T(8,128)}, ...), branch_computations={%region_2.3_spmd, %region_3.4_spmd} | conditional | flops 8619819008 | bytes 165675232 | solution.py:87
  129.7 5.2 %broadcast.54 = f32[5,512,1024]{2,1,0:T(8,128)} broadcast(f32[]{:T(128)} %constant.80.clone), dimensions={} | broadcast | bytes 10485764 | tf_op jit(solution)/shard_map/broadcast.15
  134.9 3.0 broadcast.55
  137.9 2.5 broadcast.56
  140.4 0.3 reshape.56
  140.7 0.2 broadcast.57
  141.1 0.2 copy.15
  141.4 1.8 copy-done.2
  143.2 5.3 %all_to_all.20 = f32[2,32,8,1024]{3,2,1,0:T(8,128)S(1)} all-to-all(f32[2,32,8,1024]{3,2,1,0:T(8,128)S(1)} %copy.15), channel_id=1, replica_groups=mesh['role'=2,'tile_0'=2,'tile_1'=4,'tile_2'=4,'tile_3'=2] {'tile_3'}, dimensions={0} | all-to-all | bytes 4194304 | tf_op jit(solution)/shard_map/all_to_all | solution.py:61
  148.5 1.2 reduce_sum.18
  149.7 21.2 %all_to_all.21 = f32[32,8,1024]{2,1,0:T(8,128)S(1)} all-to-all(f32[32,8,1024]{2,1,0:T(8,128)} %reduce_sum.18), channel_id=1, replica_groups=mesh['role'=2,'tile_0'=2,'tile_1'=4,'tile_2'=4,'tile_3'=2] {'tile_0','ti..., dimensions={0} | all-to-all | bytes 2097152 | tf_op jit(solution)/shard_map/all_to_all | solution.py:68
  170.9 0.1 reduce_sum.19
  171.0 1.1 broadcast_in_dim.38
  172.1 4.7 %all-to-all-start.2 = ((f32[32,8,1024]{2,1,0:T(8,128)}), f32[32,8,1024]{2,1,0:T(8,128)S(1)}, u32[]{:S(2)}, u32[]{:S(2)}) async-start(f32[32,8,1024]{2,1,0:T(8,128)} %broadcast_in_dim.38), calls=%async_computation.2 | async-start | bytes 2097152 | tf_op jit(solution)/shard_map/all_to_all | solution.py:39
  176.8 0.0 all-gather.6.cloned.1.call-start
  176.9 0.9 fusion.96
  177.8 3.4 collective-permute-start
  181.1 1.5 pad_maximum_fusion
  182.6 5.2 %copy.19 = f32[128,8,8,128]{3,1,2,0:T(8,128)} copy(f32[128,8,8,128]{3,2,1,0:T(8,128)} %bitcast.227) | data formatting | bytes 8388608
  187.8 0.8 copy.20
  188.6 3.5 collective-permute-done
  192.1 0.7 copy-done.12
  192.8 1.8 collective-permute-done.1
  194.6 3.1 concatenate.13
  197.6 3.2 conditional.3
  197.7 0.7 multiply_add_fusion
  198.4 2.5 multiply_add_fusion.1
  200.9 0.3 broadcast_in_dim.39
  201.2 9.4 %all_to_all.22 = f32[2,32,8,1024]{3,2,1,0:T(8,128)S(1)} all-to-all(f32[2,32,8,1024]{3,2,1,0:T(8,128)S(1)} %broadcast_in_dim.39), channel_id=1, replica_groups=mesh['role'=2,'tile_0'=2,'tile_1'=4,'tile_2'=4,'tile_3'=2] {'tile_3'}, dimensions={0} | all-to-all | bytes 4194304 | tf_op jit(solution)/shard_map/all_to_all | solution.py:39
  210.6 1.5 conditional.5
  210.6 0.7 broadcast.59
  211.4 0.8 reshape.58
  212.1 5.7 %maximum_select_fusion = f32[1130496]{0:T(1024)} fusion(f32[81920]{0:T(1024)S(1)} %bitcast.240, f32[1048576]{0:T(1024)} %bitcast.229, f32[81920]{0:T(1024)} %get-tuple-element.91, f32[1048576]{0:T(1024)} %copy-done.2, pred[]{:T(512)S(6)} %eq.3), kind=kLoop, calls=%fused_computation.118 | loop fusion | flops 3391488 | bytes 13565953 | tf_op jit(solution)/shard_map/jit(_where)/select_n | solution.py:167
  217.9 53.5 %collective-permute-start.2 = (f32[1130496]{0:T(1024)}, f32[1130496]{0:T(1024)}, u32[]{:S(2)}, u32[]{:S(2)}) collective-permute-start(f32[1130496]{0:T(1024)} %maximum_select_fusion), channel_id=1, source_target_pairs={{0,64},{64,0},{1,65},{65,1},{2,66},{66,2},{3,67},{67,3},{4,68},{68... | collective-permute-start | bytes 13565960 | tf_op jit(solution)/shard_map/ppermute | solution.py:79
  271.4 15.9 %all-gather.6.cloned.1.call-done = f32[1024,1024]{1,0:T(8,128)} async-done(((f32[512,1024]{1,0:T(8,128)}), f32[1024,1024]{1,0:T(8,128)}) %all-gather.6.cloned.1.call-update) | async-done | bytes 4194320 | tf_op jit(solution)/shard_map/all_gather | solution.py:27
  287.3 1.6 slice-done
  288.9 2.7 gather_fusion
  291.6 3.8 select_bitcast_fusion.1
  295.4 81.9 %collective-permute-done.2 = f32[1130496]{0:T(1024)} collective-permute-done((f32[1130496]{0:T(1024)}, f32[1130496]{0:T(1024)}, u32[]{:S(2)}, u32[]{:S(2)}) %collective-permute-start.2) | collective-permute-done | bytes 4522016 | tf_op jit(solution)/shard_map/ppermute | solution.py:79
  377.2 1.0 slice.147
  378.2 0.1 slice.135
  378.3 4.4 %slice.146 = f32[1048576]{0:T(1024)} slice(f32[1130496]{0:T(1024)} %collective-permute-done.2), slice={[0:1048576]} | slice | bytes 8388608 | tf_op jit(solution)/shard_map/slice | solution.py:170
  382.7 5.0 %slice.133 = f32[1024,1024]{1,0:T(8,128)} reshape(f32[1048576]{0:T(1024)} %slice.146) | data formatting | bytes 8388608 | tf_op jit(solution)/shard_map/slice | solution.py:170
  387.8 1.8 fusion.94
  389.5 8.7 %select_bitcast_fusion = f32[1,1024,1024]{2,1,0:T(8,128)} fusion(f32[1024,1024]{1,0:T(8,128)} %get-tuple-element.92, f32[1024,1024]{1,0:T(8,128)} %slice.133, pred[]{:T(512)S(6)} %eq.3, f32[1,1024,1024]{2,1,0:T(8,128)} %param.18), kind=kLoop, calls=%fused_computation.119 | loop fusion | flops 7340032 | bytes 16777216 | tf_op jit(solution)/shard_map/broadcast_in_dim | solution.py:183
  (25 shorter events, 0.1 us)
Async XLA Ops:
  8.0 121.7 %all-gather.4.cloned.1.call-start = ((), (), s32[]{:S(2)}) async-start(), calls=%async_computation.4 | async-start | bytes 10649600 | tf_op jit(solution)/shard_map/all_gather | solution.py:121
  141.1 2.1 copy-start.2
  170.9 5.9 %copy-start.3 = (f32[1,512,1024]{2,1,0:T(8,128)S(1)}, f32[1,512,1024]{2,1,0:T(8,128)}, u32[]{:S(2)}) copy-start(f32[1,512,1024]{2,1,0:T(8,128)} %param.13) | copy-start | bytes 6291460
  170.9 5.9 %copy-start.13 = (f32[1024]{0:T(1024)S(1)}, f32[1024]{0:T(1024)}, u32[]{:S(2)}) copy-start(f32[1024]{0:T(1024)} %param.14) | copy-start | bytes 12292
  172.1 28.8 %all-to-all-start.2 = ((f32[32,8,1024]{2,1,0:T(8,128)}), f32[32,8,1024]{2,1,0:T(8,128)S(1)}, u32[]{:S(2)}, u32[]{:S(2)}) async-start(f32[32,8,1024]{2,1,0:T(8,128)} %broadcast_in_dim.38), calls=%async_computation.2 | async-start | bytes 2097152 | tf_op jit(solution)/shard_map/all_to_all | solution.py:39
  176.8 110.5 %all-gather.6.cloned.1.call-start = ((), (), s32[]{:S(2)}) async-start(), calls=%async_computation.5 | async-start | bytes 6291456 | tf_op jit(solution)/shard_map/all_gather | solution.py:27
  177.8 14.3 %collective-permute-start = (f32[513,1]{1,0:T(8,128)}, f32[513,1]{1,0:T(8,128)S(1)}, u32[]{:S(2)}, u32[]{:S(2)}) collective-permute-start(f32[513,1]{1,0:T(8,128)} %get-tuple-element.140), channel_id=1, source_target_pairs={{0,1},{1,2},{2,3},{3,4},{4,5},{5,6},{6,7},{7,8},{8,9},{9,10},{10,1... | collective-permute-start | bytes 6164 | tf_op jit(solution)/shard_map/ppermute | solution.py:20
  181.1 13.4 %collective-permute-start.1 = (f32[513,1]{1,0:T(8,128)}, f32[513,1]{1,0:T(8,128)}, u32[]{:S(2)}, u32[]{:S(2)}) collective-permute-start(f32[513,1]{1,0:T(8,128)} %get-tuple-element.139), channel_id=1, source_target_pairs={{1,0},{2,1},{3,2},{4,3},{5,4},{6,5},{7,6},{8,7},{9,8},{10,9},{11,1... | collective-permute-start | bytes 6164 | tf_op jit(solution)/shard_map/ppermute | solution.py:21
  182.6 5.2 %copy-start.5 = (f32[1,5,16,1024]{3,2,1,0:T(8,128)S(1)}, f32[1,5,16,1024]{3,2,1,0:T(8,128)}, u32[]{:S(2)}) copy-start(f32[1,5,16,1024]{3,2,1,0:T(8,128)} %param.19) | copy-start | bytes 983044
  188.6 9.1 %copy-start.15 = (f32[1024]{0:T(1024)S(1)}, f32[1024]{0:T(1024)}, u32[]{:S(2)}) copy-start(f32[1024]{0:T(1024)} %param.15) | copy-start | bytes 12292
  192.1 0.7 copy-start.12
  210.6 1.5 copy-start.7
  212.1 59.3 %copy-start.14 = (s32[512]{0:T(512)S(1)}, s32[512]{0:T(512)}, u32[]{:S(2)}) copy-start(s32[512]{0:T(512)} %param.17) | copy-start | bytes 6148
  217.9 159.4 %collective-permute-start.2 = (f32[1130496]{0:T(1024)}, f32[1130496]{0:T(1024)}, u32[]{:S(2)}, u32[]{:S(2)}) collective-permute-start(f32[1130496]{0:T(1024)} %maximum_select_fusion), channel_id=1, source_target_pairs={{0,64},{64,0},{1,65},{65,1},{2,66},{66,2},{3,67},{67,3},{4,68},{68... | collective-permute-start | bytes 13565960 | tf_op jit(solution)/shard_map/ppermute | solution.py:79
  287.3 1.6 slice-start
  382.7 5.0 %copy-start.6 = (f32[1,5,16,1024]{3,2,1,0:T(8,128)S(1)}, f32[1,5,16,1024]{3,2,1,0:T(8,128)}, u32[]{:S(2)}) copy-start(f32[1,5,16,1024]{3,2,1,0:T(8,128)} %param.19) | copy-start | bytes 983044
Sparse Core Ops, SparseCore 0:
  11.1 118.5 all-gather.3
Sparse Core Ops, SparseCore 1:
  201.0 86.3 all-gather.5
where the time goes:
time: 407 us; the launch traced here: 406 us
  waiting for transfers between devices  223 us (55%)
  starting transfers between devices  61.7 us (15%)
  local copies, waits for them, and re-layouts  40.8 us (10%)
  blocking collectives  35.9 us (9%)
  other arithmetic  28.5 us (7%)
  between operations  15.6 us (4%)
    all_gather x1, waiting for transfers between devices, body(): full_hidden = lax.all_gather(hidden_narrow, TILE, axis=1, tiled=True)  120 us
    ppermute x1, waiting for transfers between devices, partner(): lax.ppermute(value, axis, [(i, i ^ 1 << distance) for i in range(lax.axis...  81.9 us
    ppermute x1, starting transfers between devices, partner(): lax.ppermute(value, axis, [(i, i ^ 1 << distance) for i in range(lax.axis...  53.5 us
    all_to_all x1, blocking collectives, summed_rows(): return jnp.sum(lax.all_to_all(own, far, 0, 0, tiled=True), axis=0)  21.2 us
    all_gather x1, waiting for transfers between devices, from_root(): lax.all_gather(value, axis)  15.9 us
    broadcast_in_dim x3, other arithmetic, body(): return (fields_next[None], out_next[None], hidden_next[None])  14.3 us
    another operation x5, local copies, waits for them, and re-layouts  11.7 us
    slice x2, local copies, waits for them, and re-layouts, body(): other_out = received[:out_length].reshape(own_out.shape)  9.46 us
  transfers between devices with their start and end apart: 6, of which 5 were waited for; matrix products, arithmetic and copies ran while one was open for 7% of the time, Pallas kernels for 0%

commit v1 on v0

--- a/solution.py
+++ b/solution.py
@@ -118,7 +118,9 @@
     fresh_fields = from_root(advanced, "role", 0)
     out_narrow = own_out.astype(jnp.bfloat16)
     hidden_narrow = own_hidden.astype(jnp.bfloat16)
-    full_hidden = lax.all_gather(hidden_narrow, TILE, axis=1, tiled=True)
+    full_hidden = jnp.concatenate(
+        lax.all_to_all(jnp.stack([hidden_narrow] * lax.axis_size(TILE)), TILE, 0, 0), axis=1
+    )
 
     def forward(features, full_hidden, out_narrow, target):
         inputs = []

time: 407 us -> 464 us (1.14)
  local copies, waits for them, and re-layouts: 40.8 us -> 56.6 us
  waiting for transfers between devices: 223 us -> 238 us
  blocking collectives: 35.9 us -> 48.6 us
  loops' own time: 0.23 us -> 5.68 us
  starting transfers between devices: 61.7 us -> 66.8 us
    all_to_all x0 -> x1, waiting for transfers between devices: none -> 135 us  [body(): lax.all_to_all(jnp.stack([hidden_narrow] * lax.axis_size(TILE)), TILE, 0, 0)]
    all_gather x1 -> x0, waiting for transfers between devices: 120 us -> none  [body(): full_hidden = lax.all_gather(hidden_narrow, TILE, axis=1, tiled=True)]
    all_to_all x1, blocking collectives: 21.2 us -> 33.3 us  [summed_rows(): return jnp.sum(lax.all_to_all(own, far, 0, 0, tiled=True), axis=0)]
    all_to_all x0 -> x1, starting transfers between devices: none -> 11 us  [body(): lax.all_to_all(jnp.stack([hidden_narrow] * lax.axis_size(TILE)), TILE, 0, 0)]
    all_to_all x0 -> x1, local copies, waits for them, and re-layouts: none -> 10.4 us  [body(): lax.all_to_all(jnp.stack([hidden_narrow] * lax.axis_size(TILE)), TILE, 0, 0)]
    ppermute x1, starting transfers between devices: 53.5 us -> 47.7 us  [partner(): lax.ppermute(value, axis, [(i, i ^ 1 << distance) for i in range(lax.axis...]
    another operation x3, loops' own time: 0.23 us -> 5.68 us  [guarded(): return lax.cond(flag, action, skipped, *operands)]
    another operation x5 -> x6, local copies, waits for them, and re-layouts: 11.7 us -> 17.1 us
  transfers between devices with their start and end apart: 6 -> 6, of which waited for: 5 -> 5; matrix products, arithmetic and copies ran while one was open for 7% -> 6% of each run, Pallas kernels for 0% -> 0%
where the time goes in v1:
time: 464 us; the launch traced here: 459 us
  waiting for transfers between devices  238 us (51%)
  starting transfers between devices  66.8 us (14%)
  local copies, waits for them, and re-layouts  56.6 us (12%)
  blocking collectives  48.6 us (10%)
  other arithmetic  29.5 us (6%)
  between operations  14.4 us (3%)
  loops' own time  5.68 us (1%)
    all_to_all x1, waiting for transfers between devices, body(): lax.all_to_all(jnp.stack([hidden_narrow] * lax.axis_size(TILE)), TILE, 0, 0)  135 us
    ppermute x1, waiting for transfers between devices, partner(): lax.ppermute(value, axis, [(i, i ^ 1 << distance) for i in range(lax.axis...  81.7 us
    ppermute x1, starting transfers between devices, partner(): lax.ppermute(value, axis, [(i, i ^ 1 << distance) for i in range(lax.axis...  47.7 us
    all_to_all x1, blocking collectives, summed_rows(): return jnp.sum(lax.all_to_all(own, far, 0, 0, tiled=True), axis=0)  33.3 us
    all_gather x1, waiting for transfers between devices, from_root(): lax.all_gather(value, axis)  16 us
    broadcast_in_dim x3, other arithmetic, body(): return (fields_next[None], out_next[None], hidden_next[None])  14.3 us
    another operation x5, local copies, waits for them, and re-layouts  11.7 us
    all_to_all x1, starting transfers between devices, body(): lax.all_to_all(jnp.stack([hidden_narrow] * lax.axis_size(TILE)), TILE, 0, 0)  11 us
  transfers between devices with their start and end apart: 6, of which 5 were waited for; matrix products, arithmetic and copies ran while one was open for 6% of the time, Pallas kernels for 0%

profile of v1, /device:TPU:1, one launch (start us, length us, event | category | flops | bytes accessed | tf_op | source)
XLA Modules:
  0.0 459.3 jit_solution(1391987299070624361)
XLA Ops:
  7.2 1.0 convert_bitcast_fusion
  8.2 5.4 %stack.47 = bf16[64,5,16,1024]{3,2,1,0:T(8,128)(2,1)} broadcast(bf16[5,16,1024]{2,1,0:T(8,128)(2,1)S(1)} %convert_bitcast_fusion), dimensions={1,2,3} | broadcast | bytes 10649600 | tf_op jit(solution)/shard_map/stack | solution.py:122
  13.5 11.0 %all-to-all-start = ((bf16[64,5,16,1024]{3,2,1,0:T(8,128)(2,1)}), bf16[64,5,16,1024]{3,2,1,0:T(8,128)(2,1)}, u32[]{:S(2)}, u32[]{:S(2)}) async-start(bf16[64,5,16,1024]{3,2,1,0:T(8,128)(2,1)} %stack.47), calls=%async_computation | async-start | bytes 20971520 | tf_op jit(solution)/shard_map/all_to_all | solution.py:122
  24.6 134.8 %all-to-all-done = bf16[64,5,16,1024]{3,2,1,0:T(8,128)(2,1)} async-done(((bf16[64,5,16,1024]{3,2,1,0:T(8,128)(2,1)}), bf16[64,5,16,1024]{3,2,1,0:T(8,128)(2,1)}, u32[]{:S(2)}, u32[]{:S(2)}) %all-to-all-start) | async-done | bytes 10485792 | tf_op jit(solution)/shard_map/all_to_all | solution.py:122
  159.3 10.4 %copy.16 = bf16[64,5,16,1024]{3,2,0,1:T(8,128)(2,1)} copy(bf16[64,5,16,1024]{3,2,1,0:T(8,128)(2,1)} %all-to-all-done) | data formatting | bytes 20971520 | tf_op jit(solution)/shard_map/all_to_all | solution.py:122
  169.8 16.8 %conditional.4 = (f32[5,512,1024]{2,1,0:T(8,128)}, bf16[5,512,1024]{2,1,0:T(8,128)(2,1)}, f32[1024,1024]{1,0:T(8,128)}, f32[512,1024]{1,0:T(8,128)S(1)}, f32[1048576]{0:T(1024)S(1)}) conditional(s32[]{:T(128)} %convert_element_type.58, () %tuple.54, (bf16[5,1024,1024]{2,1,0:T(8,128)(2,1)}, bf16[512,1024]{1,0:T(8,128)(2,1)S(1)}, ...), branch_computations={%region_2.3_spmd, %region_3.4_spmd} | conditional | flops 8619819008 | bytes 153092256 | solution.py:87
  169.8 5.2 %broadcast.55 = f32[5,512,1024]{2,1,0:T(8,128)} broadcast(f32[]{:T(128)} %constant.80.clone), dimensions={} | broadcast | bytes 10485764 | tf_op jit(solution)/shard_map/broadcast.15
  175.0 3.0 broadcast.56
  178.0 2.5 broadcast.57
  180.5 0.3 reshape.61
  180.8 0.2 broadcast.58
  186.5 0.2 copy.17
  186.8 1.8 copy-done.2
  188.6 5.9 %all_to_all.25 = f32[2,32,8,1024]{3,2,1,0:T(8,128)} all-to-all(f32[2,32,8,1024]{3,2,1,0:T(8,128)S(1)} %copy.17), channel_id=1, replica_groups=mesh['role'=2,'tile_0'=2,'tile_1'=4,'tile_2'=4,'tile_3'=2] {'tile_3'}, dimensions={0} | all-to-all | bytes 4194304 | tf_op jit(solution)/shard_map/all_to_all | solution.py:61
  194.6 2.8 reduce_sum.18
  197.4 33.3 %all_to_all.26 = f32[32,8,1024]{2,1,0:T(8,128)S(1)} all-to-all(f32[32,8,1024]{2,1,0:T(8,128)} %reduce_sum.18), channel_id=1, replica_groups=mesh['role'=2,'tile_0'=2,'tile_1'=4,'tile_2'=4,'tile_3'=2] {'tile_0','ti..., dimensions={0} | all-to-all | bytes 2097152 | tf_op jit(solution)/shard_map/all_to_all | solution.py:68
  230.7 0.1 reduce_sum.19
  230.7 1.1 broadcast_in_dim.38
  231.8 4.7 %all-to-all-start.3 = ((f32[32,8,1024]{2,1,0:T(8,128)}), f32[32,8,1024]{2,1,0:T(8,128)S(1)}, u32[]{:S(2)}, u32[]{:S(2)}) async-start(f32[32,8,1024]{2,1,0:T(8,128)} %broadcast_in_dim.38), calls=%async_computation.3 | async-start | bytes 2097152 | tf_op jit(solution)/shard_map/all_to_all | solution.py:39
  236.6 0.9 fusion.96
  237.5 3.4 collective-permute-start
  240.8 1.5 pad_maximum_fusion
  242.3 5.2 %copy.21 = f32[128,8,8,128]{3,1,2,0:T(8,128)} copy(f32[128,8,8,128]{3,2,1,0:T(8,128)} %bitcast.231) | data formatting | bytes 8388608
  247.5 0.8 copy.22
  248.3 3.5 collective-permute-done
  251.8 0.7 copy-done.11
  252.5 1.8 collective-permute-done.1
  254.3 3.1 concatenate.13
  257.4 3.2 conditional.3
  257.4 0.7 multiply_add_fusion
  258.1 2.5 multiply_add_fusion.1
  260.6 0.3 broadcast_in_dim.39
  260.9 9.4 %all_to_all.27 = f32[2,32,8,1024]{3,2,1,0:T(8,128)S(1)} all-to-all(f32[2,32,8,1024]{3,2,1,0:T(8,128)S(1)} %broadcast_in_dim.39), channel_id=1, replica_groups=mesh['role'=2,'tile_0'=2,'tile_1'=4,'tile_2'=4,'tile_3'=2] {'tile_3'}, dimensions={0} | all-to-all | bytes 4194304 | tf_op jit(solution)/shard_map/all_to_all | solution.py:39
  270.3 1.7 conditional.5
  270.3 0.8 broadcast.60
  271.1 0.7 reshape.63
  272.0 5.7 %maximum_select_fusion = f32[1130496]{0:T(1024)} fusion(f32[81920]{0:T(1024)S(1)} %bitcast.248, f32[1048576]{0:T(1024)} %bitcast.233, f32[81920]{0:T(1024)} %get-tuple-element.91, f32[1048576]{0:T(1024)} %copy-done.2, pred[]{:T(512)S(6)} %eq.3), kind=kLoop, calls=%fused_computation.118 | loop fusion | flops 3391488 | bytes 13565953 | tf_op jit(solution)/shard_map/jit(_where)/select_n | solution.py:169
  277.7 47.7 %collective-permute-start.2 = (f32[1130496]{0:T(1024)}, f32[1130496]{0:T(1024)}, u32[]{:S(2)}, u32[]{:S(2)}) collective-permute-start(f32[1130496]{0:T(1024)} %maximum_select_fusion), channel_id=1, source_target_pairs={{0,64},{64,0},{1,65},{65,1},{2,66},{66,2},{3,67},{67,3},{4,68},{68... | collective-permute-start | bytes 13565960 | tf_op jit(solution)/shard_map/ppermute | solution.py:79
  325.4 16.0 %all-gather.3.cloned.1.call-done = f32[1024,1024]{1,0:T(8,128)} async-done(((f32[512,1024]{1,0:T(8,128)}), f32[1024,1024]{1,0:T(8,128)}) %all-gather.3.cloned.1.call-update) | async-done | bytes 4194320 | tf_op jit(solution)/shard_map/all_gather | solution.py:27
  341.4 1.6 slice-done
  343.0 2.7 gather_fusion
  345.6 3.8 select_bitcast_fusion.1
  349.5 81.7 %collective-permute-done.2 = f32[1130496]{0:T(1024)} collective-permute-done((f32[1130496]{0:T(1024)}, f32[1130496]{0:T(1024)}, u32[]{:S(2)}, u32[]{:S(2)}) %collective-permute-start.2) | collective-permute-done | bytes 4522016 | tf_op jit(solution)/shard_map/ppermute | solution.py:79
  431.2 1.0 slice.147
  432.2 4.4 slice.146
  436.7 5.0 %slice.133 = f32[1024,1024]{1,0:T(8,128)} reshape(f32[1048576]{0:T(1024)} %slice.146) | data formatting | bytes 8388608 | tf_op jit(solution)/shard_map/slice | solution.py:172
  441.7 1.8 fusion.94
  443.5 8.7 %select_bitcast_fusion = f32[1,1024,1024]{2,1,0:T(8,128)} fusion(f32[1024,1024]{1,0:T(8,128)} %get-tuple-element.92, f32[1024,1024]{1,0:T(8,128)} %slice.133, pred[]{:T(512)S(6)} %eq.3, f32[1,1024,1024]{2,1,0:T(8,128)} %param.18), kind=kLoop, calls=%fused_computation.119 | loop fusion | flops 7340032 | bytes 16777216 | tf_op jit(solution)/shard_map/broadcast_in_dim | solution.py:185
  (28 shorter events, 0.2 us)
Async XLA Ops:
  13.5 145.8 %all-to-all-start = ((bf16[64,5,16,1024]{3,2,1,0:T(8,128)(2,1)}), bf16[64,5,16,1024]{3,2,1,0:T(8,128)(2,1)}, u32[]{:S(2)}, u32[]{:S(2)}) async-start(bf16[64,5,16,1024]{3,2,1,0:T(8,128)(2,1)} %stack.47), calls=%async_computation | async-start | bytes 20971520 | tf_op jit(solution)/shard_map/all_to_all | solution.py:122
  24.5 145.2 %copy-start.3 = (f32[1,512,1024]{2,1,0:T(8,128)S(1)}, f32[1,512,1024]{2,1,0:T(8,128)}, u32[]{:S(2)}) copy-start(f32[1,512,1024]{2,1,0:T(8,128)} %param.13) | copy-start | bytes 6291460
  24.6 145.2 %copy-start.7 = (bf16[512,1024]{1,0:T(8,128)(2,1)S(1)}, bf16[512,1024]{1,0:T(8,128)(2,1)}, u32[]{:S(2)}) copy-start(bf16[512,1024]{1,0:T(8,128)(2,1)} %param.16) | copy-start | bytes 3145732
  186.5 2.1 copy-start.2
  230.7 5.9 %copy-start.12 = (f32[1024]{0:T(1024)S(1)}, f32[1024]{0:T(1024)}, u32[]{:S(2)}) copy-start(f32[1024]{0:T(1024)} %param.14) | copy-start | bytes 12292
  231.8 28.8 %all-to-all-start.3 = ((f32[32,8,1024]{2,1,0:T(8,128)}), f32[32,8,1024]{2,1,0:T(8,128)S(1)}, u32[]{:S(2)}, u32[]{:S(2)}) async-start(f32[32,8,1024]{2,1,0:T(8,128)} %broadcast_in_dim.38), calls=%async_computation.3 | async-start | bytes 2097152 | tf_op jit(solution)/shard_map/all_to_all | solution.py:39
  236.6 104.8 %all-gather.3.cloned.1.call-start = ((), (), s32[]{:S(2)}) async-start(), calls=%async_computation.5 | async-start | bytes 6291456 | tf_op jit(solution)/shard_map/all_gather | solution.py:27
  237.5 14.3 %collective-permute-start = (f32[513,1]{1,0:T(8,128)}, f32[513,1]{1,0:T(8,128)S(1)}, u32[]{:S(2)}, u32[]{:S(2)}) collective-permute-start(f32[513,1]{1,0:T(8,128)} %get-tuple-element.140), channel_id=1, source_target_pairs={{0,1},{1,2},{2,3},{3,4},{4,5},{5,6},{6,7},{7,8},{8,9},{9,10},{10,1... | collective-permute-start | bytes 6164 | tf_op jit(solution)/shard_map/ppermute | solution.py:20
  240.8 13.5 %collective-permute-start.1 = (f32[513,1]{1,0:T(8,128)}, f32[513,1]{1,0:T(8,128)}, u32[]{:S(2)}, u32[]{:S(2)}) collective-permute-start(f32[513,1]{1,0:T(8,128)} %get-tuple-element.139), channel_id=1, source_target_pairs={{1,0},{2,1},{3,2},{4,3},{5,4},{6,5},{7,6},{8,7},{9,8},{10,9},{11,1... | collective-permute-start | bytes 6164 | tf_op jit(solution)/shard_map/ppermute | solution.py:21
  242.3 5.2 %copy-start.4 = (f32[1,5,16,1024]{3,2,1,0:T(8,128)S(1)}, f32[1,5,16,1024]{3,2,1,0:T(8,128)}, u32[]{:S(2)}) copy-start(f32[1,5,16,1024]{3,2,1,0:T(8,128)} %param.19) | copy-start | bytes 983044
  248.3 9.1 %copy-start.14 = (f32[1024]{0:T(1024)S(1)}, f32[1024]{0:T(1024)}, u32[]{:S(2)}) copy-start(f32[1024]{0:T(1024)} %param.15) | copy-start | bytes 12292
  251.8 0.7 copy-start.11
  270.3 1.7 copy-start.6
  272.0 53.4 %copy-start.13 = (s32[512]{0:T(512)S(1)}, s32[512]{0:T(512)}, u32[]{:S(2)}) copy-start(s32[512]{0:T(512)} %param.17) | copy-start | bytes 6148
  277.7 153.4 %collective-permute-start.2 = (f32[1130496]{0:T(1024)}, f32[1130496]{0:T(1024)}, u32[]{:S(2)}, u32[]{:S(2)}) collective-permute-start(f32[1130496]{0:T(1024)} %maximum_select_fusion), channel_id=1, source_target_pairs={{0,64},{64,0},{1,65},{65,1},{2,66},{66,2},{3,67},{67,3},{4,68},{68... | collective-permute-start | bytes 13565960 | tf_op jit(solution)/shard_map/ppermute | solution.py:79
  341.4 1.6 slice-start
  436.7 5.0 %copy-start.5 = (f32[1,5,16,1024]{3,2,1,0:T(8,128)S(1)}, f32[1,5,16,1024]{3,2,1,0:T(8,128)}, u32[]{:S(2)}) copy-start(f32[1,5,16,1024]{3,2,1,0:T(8,128)} %param.19) | copy-start | bytes 983044
Sparse Core Ops, SparseCore 0:
  260.7 80.6 all-gather.2
